TPU v7x, 32 devices: a whole 2x2x4 slice. The times are simulated.
32 devices in a mesh: ens: 2 (over y), tile: 4 (over z), section: 2 (over x), chan: 2 (over core).
Axes of the slice: x: 2, y: 2, z: 4, core: 2. Of those that a mesh axis runs over, the one named last changes fastest.
Arguments:
- activation: bfloat16 [2, 192, 14, 14, 192], P('section', ('ens', 'tile'), None, None, 'chan'), parts along dimension 1, may hold values from -6 to 6
- boundary: bfloat16 [2, 192, 14, 14, 192], P('section', ('ens', 'tile'), None, None, 'chan'), parts along dimension 1, may hold values from -6 to 6
- conv_weight: bfloat16 [2, 5, 192, 192], P('section', None, None, 'chan'), may hold values from -0.1875 to 0.1875
- neighbours: int32 [96, 4], replicated, may hold values from 0 to 95, as said below
- rotations: int32 [96, 4], replicated, may hold values from 0 to 3, as said below
Outputs:
- input_grad: bfloat16 [2, 192, 14, 14, 192], P('section', ('ens', 'tile'), None, None, 'chan'), parts along dimension 1
- weight_grad: float32 [2, 10, 192, 192], P('section', 'ens', 'tile', 'chan'), parts along dimension 1
There are 2 independent parts, one for each index of `ens`. A program takes and returns all parts, laid end to end along the dimension named above; an argument that names none is the same for every part. Nothing has to cross between parts.
Inputs may be any that keep to these rules, and one draw needn't show every extreme that they name: The 96 tiles are those of a cube whose faces hold equal square grids of tiles, stored in a drawn order and each turned by a drawn number of quarter turns; neighbours name the four tiles beside a tile's edges, four different ones, and every tile is named four times. `rotations`: turning tile neighbours[t, k] by this many quarter turns makes its cells continue tile t's across edge k.
All inputs are finite; a program needn't handle non-finite values.
Results may differ from a plain program's by a relative error of at most 0.003.
Values may be sent and summed in bfloat16 or wider, within the bound.
A program may use at most 128 MiB of HBM per device.

v0:
```python
import jax
import jax.numpy as jnp
from jax import lax
from jax.sharding import PartitionSpec as P

TAP_OFFSETS = ((0, 0), (-1, 0), (0, -1), (1, 0), (0, 1))


def from_behind(value, axis, by):
    size = lax.axis_size(axis)
    return lax.ppermute(value, axis, [(i, (i + by) % size) for i in range(size)])


def tile_edges(field):
    return jnp.stack([field[:, 0], field[:, :, 0], field[:, -1], field[:, :, -1]], axis=1)


def border_field(field, strips):
    padded = jnp.pad(field, ((0, 0), (1, 1), (1, 1), (0, 0)))
    padded = padded.at[:, 0, 1:-1].set(strips[:, 0])
    padded = padded.at[:, 1:-1, 0].set(strips[:, 1])
    padded = padded.at[:, -1, 1:-1].set(strips[:, 2])
    padded = padded.at[:, 1:-1, -1].set(strips[:, 3])
    return padded


def shifted_view(padded, offset, tile_side):
    row_shift, col_shift = offset
    return padded[
        :, 1 - row_shift : 1 - row_shift + tile_side, 1 - col_shift : 1 - col_shift + tile_side
    ]


def body(activation, boundary, conv_weight, neighbours, rotations):
    saved_input = activation[0]
    upstream = from_behind(boundary, "section", -1)[0]
    weights = conv_weight[0]
    tiles_here = saved_input.shape[0]
    tile_side = saved_input.shape[1]
    start_tile = lax.axis_index("tile") * tiles_here
    adjacent = lax.dynamic_slice_in_dim(neighbours, start_tile, tiles_here, 0)
    quarter_turns = lax.dynamic_slice_in_dim(rotations, start_tile, tiles_here, 0)
    side_index = jnp.arange(4, dtype=jnp.int32)[None, :]
    source = (side_index + 2 - quarter_turns) % 4
    flipped = (
        (quarter_turns == 2)
        | (quarter_turns == 1) & (source % 2 == 0)
        | (quarter_turns == 3) & (source % 2 == 1)
    )
    every_edge = lax.all_gather(tile_edges(upstream), "tile", axis=0, tiled=True)
    strips = every_edge[adjacent, source]
    strips = jnp.where(flipped[:, :, None, None], jnp.flip(strips, axis=2), strips)
    grad_pad = border_field(upstream, strips)
    half_input, half_pad = (
        lax.all_to_all(saved_input, "chan", split_axis=0, concat_axis=3, tiled=True),
        lax.all_to_all(grad_pad, "chan", split_axis=0, concat_axis=3, tiled=True),
    )
    weight_full = lax.all_gather(weights, "chan", axis=2, tiled=True)
    floats = half_input.astype(jnp.float32)
    logistic = jax.nn.sigmoid(floats)
    activated = (floats * logistic).astype(jnp.bfloat16)
    half_views = [
        shifted_view(half_pad, TAP_OFFSETS[tap_index], tile_side) for tap_index in range(5)
    ]
    act_grad = jnp.zeros(floats.shape, jnp.float32)
    for tap_index in range(5):
        act_grad = act_grad + jnp.einsum(
            "tijo,co->tijc",
            half_views[tap_index],
            weight_full[tap_index],
            preferred_element_type=jnp.float32,
        )
    derivative = logistic * (1.0 + floats * (1.0 - logistic))
    half_grad = (derivative * act_grad).astype(jnp.bfloat16)
    input_grad = lax.all_to_all(half_grad, "chan", split_axis=3, concat_axis=0, tiled=True)
    full_terms = jnp.stack(
        [
            jnp.einsum(
                "tijc,tijo->co",
                activated,
                half_views[tap_index],
                preferred_element_type=jnp.float32,
            )
            for tap_index in range(5)
        ]
    )
    local_terms = lax.psum_scatter(full_terms, "chan", scatter_dimension=2, tiled=True)
    shared = lax.psum_scatter(local_terms, "tile", scatter_dimension=1, tiled=True)
    normalizer = float(tiles_here * lax.axis_size("tile") * tile_side * tile_side) ** (-0.5)
    return (input_grad[None], (shared * normalizer)[None])


def solution(mesh):
    return jax.shard_map(
        body,
        mesh=mesh,
        in_specs=(
            P("section", ("ens", "tile"), None, None, "chan"),
            P("section", ("ens", "tile"), None, None, "chan"),
            P("section", None, None, "chan"),
            P(),
            P(),
        ),
        out_specs=(
            P("section", ("ens", "tile"), None, None, "chan"),
            P("section", "ens", "tile", "chan"),
        ),
        check_vma=False,
    )
```

profile of v0, /device:TPU:1, one launch (start us, length us, event | category | flops | bytes accessed | tf_op | source)
XLA Modules:
  0.0 172.3 jit_solution(13334766695314406877)
XLA Ops:
  7.2 2.1 %collective-permute-start = (bf16[1,24,14,14,96]{4,1,3,2,0:T(8,128)(2,1)}, bf16[1,24,14,14,96]{4,1,3,2,0:T(8,128)(2,1)}, u32[]{:S(2)}, u32[]{:S(2)}) collective-permute-start(bf16[1,24,14,14,96]{4,1,3,2,0:T(8,128)(2,1)} %param.14), channel_id=1, source_target_pairs={{0,2},{2,0},{1,3},{3,1},{4,6},{6,4},{5,7},{7,5},{8,10},{10,8},{9,1... | collective-permute-start | bytes 2709512 | tf_op jit(solution)/shard_map/ppermute | solution.py:11
  9.3 2.6 %copy.141 = bf16[1,24,14,14,96]{4,3,2,1,0:T(8,128)(2,1)} copy(bf16[1,24,14,14,96]{4,1,3,2,0:T(8,128)(2,1)} %param.13) | data formatting | bytes 1806336 | tf_op args[0]
  11.9 4.7 %all-to-all-start = ((bf16[24,14,14,96]{3,2,1,0:T(8,128)(2,1)}), bf16[24,14,14,96]{3,2,1,0:T(8,128)(2,1)S(1)}, u32[]{:S(2)}, u32[]{:S(2)}) async-start(bf16[24,14,14,96]{3,2,1,0:T(8,128)(2,1)} %bitcast.114), calls=%async_computation | async-start | bytes 2752512 | tf_op jit(solution)/shard_map/all_to_all | solution.py:55
  16.9 1.7 all-to-all-done
  18.6 0.3 convert_bitcast_fusion
  18.9 3.3 %copy.51 = f32[12,14,14,2,96]{4,3,2,1,0:T(2,128)} copy(f32[12,14,14,2,96]{4,2,1,0,3:T(8,128)S(1)} %convert_bitcast_fusion) | data formatting | bytes 3612672 | tf_op jit(solution)/shard_map/convert_element_type | solution.py:59
  22.2 3.2 %reshape.182 = f32[12,14,14,192]{3,2,1,0:T(8,128)S(1)} reshape(f32[12,14,14,2,96]{4,3,2,1,0:T(2,128)} %copy.51) | data formatting | bytes 3612672 | tf_op jit(solution)/shard_map/convert_element_type | solution.py:59
  25.5 0.3 copy.62
  25.8 2.5 %all-gather = bf16[1,5,192,192]{2,1,0,3:T(8,128)(2,1)} all-gather(bf16[1,5,192,96]{2,1,0,3:T(8,128)(2,1)S(1)} %copy.62), channel_id=2, replica_groups=mesh['ens'=2,'tile'=4,'section'=2,'chan'=2] {'chan'}, dimensions={3}, use_global_device_ids=true | all-gather | bytes 552960 | tf_op jit(solution)/shard_map/all_gather | solution.py:58
  28.3 0.6 fusion.71
  29.0 1.8 %multiply_convert_fusion = bf16[12,14,14,192]{3,2,1,0:T(8,128)(2,1)} fusion(f32[12,14,14,192]{3,2,1,0:T(8,128)S(1)} %reshape.182), kind=kLoop, calls=%fused_computation.2 | loop fusion | flops 2257920 | bytes 2709504 | tf_op jit(solution)/shard_map/convert_element_type | solution.py:61
  30.8 5.0 %collective-permute-done = bf16[1,24,14,14,96]{4,1,3,2,0:T(8,128)(2,1)} collective-permute-done((bf16[1,24,14,14,96]{4,1,3,2,0:T(8,128)(2,1)}, bf16[1,24,14,14,96]{4,1,3,2,0:T(8,128)(2,1)}, u32[]{:S(2)}, u32[]{:S(2)}) %collective-permute-start) | collective-permute-done | bytes 903200 | tf_op jit(solution)/shard_map/ppermute | solution.py:11
  35.8 0.9 fusion.69
  36.8 1.0 slice_bitcast_fusion.3
  38.0 24.4 %all_gather.6 = bf16[96,4,14,96]{3,1,2,0:T(4,128)(2,1)S(1)} all-gather(bf16[24,4,14,96]{3,1,2,0:T(4,128)(2,1)S(1)} %copy.53), channel_id=1, replica_groups=mesh['ens'=2,'tile'=4,'section'=2,'chan'=2] {'tile'}, dimensions={0}, use_global_device_ids=true | all-gather | bytes 1290240 | tf_op jit(solution)/shard_map/all_gather | solution.py:50
  62.4 0.4 copy.55
  62.9 1.2 gather_fusion
  64.3 1.6 pad.20
  66.1 1.3 slice_dynamic-update-slice_fusion.1
  67.5 1.0 copy.59
  68.5 8.1 %all_to_all.42 = bf16[24,16,16,96]{3,1,2,0:T(8,128)(2,1)S(1)} all-to-all(bf16[24,16,16,96]{3,1,2,0:T(8,128)(2,1)S(1)} %copy.59), channel_id=1, replica_groups=mesh['ens'=2,'tile'=4,'section'=2,'chan'=2] {'chan'}, dimensions={0} | all-to-all | bytes 2359296 | tf_op jit(solution)/shard_map/all_to_all | solution.py:56
  76.7 1.6 copy.61
  78.3 1.0 all_to_all.35
  79.3 1.8 %fusion.68 = (bf16[12,14,14,192]{3,2,1,0:T(8,128)(2,1)S(1)}, bf16[12,14,14,192]{3,2,1,0:T(8,128)(2,1)S(1)}, bf16[12,14,14,192]{3,2,1,0:T(8,128)(2,1)S(1)}, bf16[...) fusion(bf16[12,16,16,192]{3,2,1,0:T(8,128)(2,1)S(1)} %all_to_all.35), kind=kLoop, calls=%fused_computation.73 | loop fusion | bytes 9031680 | tf_op jit(solution)/shard_map/slice | solution.py:29
  81.2 1.3 fusion.13
  82.4 1.3 fusion.19
  83.7 1.3 fusion.25
  84.9 1.3 fusion.31
  86.2 1.3 fusion.37
  87.4 2.0 %copy.92 = f32[5,192,192]{1,0,2:T(8,128)S(1)} copy(f32[5,192,192]{2,1,0:T(8,128)} %fusion.37) | data formatting | bytes 1474560
  89.4 1.2 reshape.223
  90.7 0.3 reduce-scatter.5.cloned.1.call-start
  91.0 0.8 copy-done.1
  91.8 0.7 fusion.70
  93.2 2.1 %fusion.48 = f32[12,14,14,192]{3,2,1,0:T(8,128)} fusion(bf16[1,1,192,192]{3,2,1,0:T(8,128)(2,1)S(1)} %copy.97, bf16[12,16,16,192]{3,2,1,0:T(8,128)(2,1)S(1)} %all_to_all.35), kind=kOutput, calls=%fused_computation.37 | convolution fusion | flops 173408256 | bytes 3280896 | tf_op jit(solution)/shard_map/tijo,co->tijc/dot_general | solution.py:67
  95.3 2.2 %fusion.50 = f32[12,14,14,192]{3,2,1,0:T(8,128)} fusion(bf16[1,1,192,192]{3,2,1,0:T(8,128)(2,1)S(1)} %copy.96, bf16[12,16,16,192]{3,2,1,0:T(8,128)(2,1)S(1)} %all_to_all.35), kind=kOutput, calls=%fused_computation.39 | convolution fusion | flops 173408256 | bytes 3280896 | tf_op jit(solution)/shard_map/tijo,co->tijc/dot_general | solution.py:67
  97.5 2.1 %fusion.52 = f32[12,14,14,192]{3,2,1,0:T(8,128)} fusion(bf16[1,1,192,192]{3,2,1,0:T(8,128)(2,1)S(1)} %copy.95, bf16[12,16,16,192]{3,2,1,0:T(8,128)(2,1)S(1)} %all_to_all.35), kind=kOutput, calls=%fused_computation.41 | convolution fusion | flops 173408256 | bytes 3280896 | tf_op jit(solution)/shard_map/tijo,co->tijc/dot_general | solution.py:67
  99.7 2.1 %fusion.46 = f32[12,14,14,192]{3,2,1,0:T(8,128)} fusion(bf16[1,1,192,192]{3,2,1,0:T(8,128)(2,1)S(1)} %copy.98, bf16[12,16,16,192]{3,2,1,0:T(8,128)(2,1)S(1)} %all_to_all.35), kind=kOutput, calls=%fused_computation.35 | convolution fusion | flops 173408256 | bytes 3280896 | tf_op jit(solution)/shard_map/tijo,co->tijc/dot_general | solution.py:67
  101.8 1.2 reshape.224
  103.0 1.1 copy.93
  104.1 6.4 %multiply_convert_fusion.1 = bf16[12,14,14,192]{3,2,1,0:T(8,128)(2,1)S(1)} fusion(f32[12,14,14,192]{3,2,1,0:T(8,128)} %fusion.46, f32[12,14,14,192]{3,2,1,0:T(8,128)} %fusion.48, f32[12,14,14,192]{3,2,1,0:T(8,128)} %fusion.52, f32[12,14,14,192]{3,2,1,0:T(8,128)} %fusion.50, f32[12,14,14,192]{3,2,1,0:T(8,128)} %copy-done, ...), kind=kOutput, calls=%fused_computation.3 | convolution fusion | flops 179278848 | bytes 11409408 | tf_op jit(solution)/shard_map/tijo,co->tijc/dot_general | solution.py:67
  110.5 7.7 %copy.68 = bf16[12,14,14,192]{2,1,0,3:T(8,128)(2,1)} copy(bf16[12,14,14,192]{3,2,1,0:T(8,128)(2,1)S(1)} %multiply_convert_fusion.1) | data formatting | bytes 1806336 | tf_op jit(solution)/shard_map/convert_element_type | solution.py:74
  118.2 14.8 %reshape.225 = bf16[2,2,112896]{2,1,0:T(2,128)(2,1)S(1)} reshape(bf16[192,12,14,14]{3,2,1,0:T(8,128)(2,1)} %bitcast.115) | data formatting | bytes 1806336
  133.0 4.5 %all_to_all.43 = bf16[2,2,112896]{2,1,0:T(2,128)(2,1)S(1)} all-to-all(bf16[2,2,112896]{2,1,0:T(2,128)(2,1)S(1)} %reshape.225), channel_id=1, replica_groups=mesh['ens'=2,'tile'=4,'section'=2,'chan'=2] {'chan'}, dimensions={0} | all-to-all | bytes 1806336 | tf_op jit(solution)/shard_map/all_to_all | solution.py:75
  137.6 15.1 %reshape.226 = bf16[192,12,14,14]{3,2,1,0:T(8,128)(2,1)} reshape(bf16[2,2,112896]{2,1,0:T(2,128)(2,1)S(1)} %all_to_all.43) | data formatting | bytes 1806336
  152.6 9.8 %copy.69 = bf16[12,14,14,2,96]{4,2,1,0,3:T(8,128)(2,1)S(1)} copy(bf16[12,14,14,2,96]{2,1,0,4,3:T(8,128)(2,1)} %bitcast.116) | data formatting | bytes 1806336 | tf_op jit(solution)/shard_map/all_to_all | solution.py:75
  162.4 1.5 copy.80
  163.9 1.6 multiply_bitcast_fusion
  (34 shorter events, 1.8 us)
Async XLA Ops:
  7.2 28.6 %collective-permute-start = (bf16[1,24,14,14,96]{4,1,3,2,0:T(8,128)(2,1)}, bf16[1,24,14,14,96]{4,1,3,2,0:T(8,128)(2,1)}, u32[]{:S(2)}, u32[]{:S(2)}) collective-permute-start(bf16[1,24,14,14,96]{4,1,3,2,0:T(8,128)(2,1)} %param.14), channel_id=1, source_target_pairs={{0,2},{2,0},{1,3},{3,1},{4,6},{6,4},{5,7},{7,5},{8,10},{10,8},{9,1... | collective-permute-start | bytes 2709512 | tf_op jit(solution)/shard_map/ppermute | solution.py:11
  11.9 4.7 %copy-start.4 = (s32[96,4]{0,1:T(4,128)S(1)}, s32[96,4]{0,1:T(4,128)}, u32[]{:S(2)}) copy-start(s32[96,4]{0,1:T(4,128)} %param.17) | copy-start | bytes 4612
  11.9 4.7 %copy-start.5 = (s32[96,4]{0,1:T(4,128)S(1)}, s32[96,4]{0,1:T(4,128)}, u32[]{:S(2)}) copy-start(s32[96,4]{0,1:T(4,128)} %param.16) | copy-start | bytes 4612
  11.9 6.7 %all-to-all-start = ((bf16[24,14,14,96]{3,2,1,0:T(8,128)(2,1)}), bf16[24,14,14,96]{3,2,1,0:T(8,128)(2,1)S(1)}, u32[]{:S(2)}, u32[]{:S(2)}) async-start(bf16[24,14,14,96]{3,2,1,0:T(8,128)(2,1)} %bitcast.114), calls=%async_computation | async-start | bytes 2752512 | tf_op jit(solution)/shard_map/all_to_all | solution.py:55
  16.6 85.2 %reduce-scatter.7.cloned.1.call-start = ((), (), s32[]{:S(2)}) async-start(), calls=%async_computation.6 | async-start | bytes 1179648
  22.2 3.2 %copy-start.3 = (bf16[1,5,192,96]{3,2,1,0:T(8,128)(2,1)S(1)}, bf16[1,5,192,96]{3,2,1,0:T(8,128)(2,1)}, u32[]{:S(2)}) copy-start(bf16[1,5,192,96]{3,2,1,0:T(8,128)(2,1)} %param.15) | copy-start | bytes 552964
  25.5 5.4 %copy-start = (f32[12,14,14,192]{3,2,1,0:T(8,128)}, f32[12,14,14,192]{3,2,1,0:T(8,128)S(1)}, u32[]{:S(2)}) copy-start(f32[12,14,14,192]{3,2,1,0:T(8,128)S(1)} %reshape.182) | copy-start | bytes 5419012
  79.3 1.8 %copy-start.2 = (bf16[12,14,14,192]{3,2,1,0:T(8,128)(2,1)S(1)}, bf16[12,14,14,192]{3,2,1,0:T(8,128)(2,1)}, u32[]{:S(2)}) copy-start(bf16[12,14,14,192]{3,2,1,0:T(8,128)(2,1)} %multiply_convert_fusion) | copy-start | bytes 2709508
  90.7 1.1 copy-start.1
  90.7 73.2 %reduce-scatter.5.cloned.1.call-start = ((), (), s32[]{:S(2)}) async-start(), calls=%async_computation.5 | async-start | bytes 614400 | tf_op jit(solution)/shard_map/reduce_scatter | solution.py:88
Sparse Core Ops, SparseCore 0:
  90.8 9.1 reduce-scatter.6
  104.2 20.3 reduce-scatter.4
where the time goes:
time: 173 us; the launch traced here: 172 us
  local copies, waits for them, and re-layouts  79.2 us (46%)
  blocking collectives  39.6 us (23%)
  matrix products  21.3 us (12%)
  between operations  14.3 us (8%)
  starting transfers between devices  7.08 us (4%)
  waiting for transfers between devices  6.71 us (4%)
  other arithmetic  4.15 us (2%)
    unnamed x26, local copies, waits for them, and re-layouts  41.3 us
    all_gather x1, blocking collectives, body(): lax.all_gather(tile_edges(upstream), 'tile', axis=0, tiled=True)  24.4 us
    dot_general x5, matrix products, body(): jnp.einsum('tijo,co->tijc', half_views[tap_index], weight_full[tap_index]...  15 us
    all_to_all x1, local copies, waits for them, and re-layouts, body(): lax.all_to_all(half_grad, 'chan', split_axis=3, concat_axis=0, tiled=True)  9.79 us
    all_to_all x1, blocking collectives, body(): lax.all_to_all(grad_pad, 'chan', split_axis=0, concat_axis=3, tiled=True)  8.13 us
    convert_element_type x1, local copies, waits for them, and re-layouts, body(): half_grad = (derivative * act_grad).astype(jnp.bfloat16)  7.71 us
    convert_element_type x2, local copies, waits for them, and re-layouts, body(): floats = half_input.astype(jnp.float32)  6.53 us
    dot_general x5, matrix products, body(): jnp.einsum('tijc,tijo->co', activated, half_views[tap_index], preferred_e...  6.29 us
  transfers between devices with their start and end apart: 4, of which 2 were waited for; matrix products, arithmetic and copies ran while one was open for 45% of the time, Pallas kernels for 0%

commit v1 on v0

v1 whole, which is shorter than its diff:
```python
import functools

import jax
import jax.numpy as jnp
from jax import lax
from jax.experimental import pallas as pl
from jax.experimental.pallas import tpu as pltpu
from jax.sharding import PartitionSpec as P

MESH = pl.DeviceIdType.MESH
LANES = 128
F32 = jnp.float32
BF16 = jnp.bfloat16


def flat(x):
    return x.reshape(-1, x.shape[-1])


def kernel(
    n_tile, n_section, normalizer,
    act_ref, bnd_ref, w_ref, idx_ref,
    grad_ref, wg_ref,
    peri_src, inner_src, ring, inner, third, pad, wother, wfull, activ, deriv, acc, wsend, wrecv,
    x_send, x_recv, z_send, z_recv, w_sems, c_send, c_recv, h_send, h_recv, g_send, g_recv,
):
    ens, me, sec, chan = (lax.axis_index(a) for a in ("ens", "tile", "section", "chan"))
    side, _, tiles, ch = act_ref.shape
    full = side - 1
    half_tiles = n_tile // 2
    other = 1 - chan
    sibling = (ens, me, sec, other)
    target = (ens, me, lax.rem(sec + n_section - 1, n_section), chan)
    source = (ens, me, lax.rem(sec + 1, n_section), chan)
    lead = ch // 3

    def remote(src, dst, ss, rs, dev):
        return pltpu.make_async_remote_copy(
            src_ref=src, dst_ref=dst, send_sem=ss, recv_sem=rs, device_id=dev, device_id_type=MESH
        )

    barrier = pltpu.get_barrier_semaphore()
    for dev in (sibling, target, source):
        pl.semaphore_signal(barrier, inc=1, device_id=dev, device_id_type=MESH)
    for step in range(1, n_tile):
        for k in range(2):
            dev = (ens, lax.rem(me + step, n_tile), sec, k)
            pl.semaphore_signal(barrier, inc=1, device_id=dev, device_id_type=MESH)

    rows_i = lax.broadcasted_iota(jnp.int32, (ch, LANES), 0)
    cols_i = lax.broadcasted_iota(jnp.int32, (ch, LANES), 1)
    eye = (rows_i == cols_i).astype(BF16)
    picks = [
        ((cols_i >= ch) & (rows_i - b * lead == cols_i - ch)).astype(BF16) for b in range(3)
    ]

    def pack(groups, store):
        tail = groups[3]
        for b in range(3):
            out = jnp.dot(groups[b], eye, preferred_element_type=F32) + jnp.dot(
                tail, picks[b], preferred_element_type=F32
            )
            store(b, out.astype(BF16).reshape(-1, tiles, LANES))

    wide_i = lax.broadcasted_iota(jnp.int32, (LANES, LANES), 0)
    wide_j = lax.broadcasted_iota(jnp.int32, (LANES, LANES), 1)
    moves = [
        ((wide_i >= ch) & (wide_j == wide_i - ch + b * lead)).astype(BF16) for b in range(3)
    ]

    def untail(blocks):
        total = jnp.dot(blocks[0], moves[0], preferred_element_type=F32)
        for b in range(1, 3):
            total = total + jnp.dot(blocks[b], moves[b], preferred_element_type=F32)
        return total.astype(BF16)

    def keep(x):
        lane = lax.broadcasted_iota(jnp.int32, x.shape, x.ndim - 1)
        return jnp.where(lane < ch, x.astype(F32), 0.0).astype(BF16)

    def put_peri(b, x):
        peri_src[b] = x

    pack(
        [
            flat(bnd_ref[0, 0:full]),
            flat(bnd_ref[0:full, full]),
            flat(bnd_ref[full, 1 : full + 1]),
            flat(bnd_ref[1 : full + 1, 0]),
        ],
        put_peri,
    )
    pl.semaphore_wait(barrier, 3 + 2 * (n_tile - 1))
    send_peri = remote(peri_src, ring.at[me], x_send.at[0], x_recv.at[0], target)
    send_peri.start()
    mine_c = pl.multiple_of(chan * ch, 16)
    other_c = pl.multiple_of(other * ch, 16)
    send_w = remote(w_ref.at[:, pl.ds(other_c, ch), :], wother, w_sems.at[0], w_sems.at[1], sibling)
    send_w.start()
    n_chunk = inner.shape[0]
    sends_inner = []
    for m in range(n_chunk):
        first = 1 + 4 * m

        def put_inner(b, x, m=m):
            inner_src[m, b] = x

        pack([flat(bnd_ref[first + g, 1:full]) for g in range(4)], put_inner)
        copy = remote(
            inner_src.at[m], inner.at[m], x_send.at[1 + m], x_recv.at[1 + m], target
        )
        copy.start()
        sends_inner.append(copy)

    acc[...] = jnp.zeros_like(acc)

    def silu_row(i, carry):
        v = act_ref[i].astype(F32)
        logistic = 1.0 / (1.0 + jnp.exp(-v))
        activ[i] = (v * logistic).astype(BF16)
        deriv[i] = logistic * (1.0 + v * (1.0 - logistic))
        return carry

    lax.fori_loop(0, side, silu_row, 0)
    wfull[...] = jnp.zeros_like(wfull)
    wfull[:, :, 0:ch] = w_ref[:, pl.ds(mine_c, ch), :]
    send_w.wait()
    wfull[:, :, LANES : LANES + ch] = wother[...]

    send_peri.wait()
    sends_z = []
    for step in range(1, n_tile):
        dev = (ens, lax.rem(me + step, n_tile), sec, chan)
        copy = remote(ring.at[me], ring.at[me], z_send.at[step - 1], z_recv.at[step - 1], dev)
        copy.start()
        sends_z.append(copy)
    blocks = [ring[me, b] for b in range(3)]
    tail = untail([flat(x) for x in blocks]).reshape(-1, tiles, LANES)
    pad[1, 1 : full + 1, :, 0:LANES] = keep(blocks[0])
    pad[1 : full + 1, full + 1, :, 0:LANES] = keep(blocks[1])
    pad[full + 1, 2 : full + 2, :, 0:LANES] = keep(blocks[2])
    pad[2 : full + 2, 1, :, 0:LANES] = tail

    def to_sibling(rows, cols, ss, rs):
        return remote(
            pad.at[rows, cols, :, 0:LANES], pad.at[rows, cols, :, LANES : 2 * LANES], ss, rs, sibling
        )

    inside = pl.ds(1, side)
    sends_c = [
        to_sibling(pl.ds(1, 1), inside, c_send.at[n_chunk], c_recv.at[n_chunk]),
        to_sibling(pl.ds(side, 1), inside, c_send.at[n_chunk + 1], c_recv.at[n_chunk + 1]),
    ]
    for copy in sends_c:
        copy.start()
    for m in range(n_chunk):
        sends_inner[m].wait()
        first = 2 + 4 * m
        blocks = [inner[m, b] for b in range(3)]
        for b in range(3):
            pad[first + b, 2 : full + 1, :, 0:LANES] = keep(blocks[b])
        pad[first + 3, 2 : full + 1, :, 0:LANES] = untail([flat(x) for x in blocks]).reshape(
            -1, tiles, LANES
        )
        copy = to_sibling(pl.ds(first, 4), inside, c_send.at[m], c_recv.at[m])
        copy.start()
        sends_c.append(copy)

    for copy in sends_z:
        copy.wait()
    for z in range(n_tile):
        third[z] = untail([flat(ring[z, b]) for b in range(3)]).reshape(-1, tiles, LANES)

    def edge(s, p):
        if s == 0:
            part = ring[:, 0, p] if p < full else ring[:, 1, 0]
        elif s == 3:
            part = ring[:, 1, p] if p < full else ring[:, 2, full - 1]
        elif s == 2:
            part = third[:, full - 1] if p == 0 else ring[:, 2, p - 1]
        else:
            part = ring[:, 0, 0] if p == 0 else third[:, p - 1]
        return flat(part)

    n_all = n_tile * tiles
    which = idx_ref[...]
    spots = lax.broadcasted_iota(jnp.int32, (4 * tiles, 4 * n_all), 1)
    plain = (which == spots).astype(F32).astype(BF16)
    turned = (which == spots + 4 * n_all).astype(F32).astype(BF16)
    for p in range(side):
        ahead = jnp.concatenate([edge(s, p) for s in range(4)], axis=0)
        behind = jnp.concatenate([edge(s, full - p) for s in range(4)], axis=0)
        strip = jnp.dot(plain, ahead, preferred_element_type=F32) + jnp.dot(
            turned, behind, preferred_element_type=F32
        )
        strip = keep(strip).reshape(4, tiles, LANES)
        pad[0, 1 + p, :, 0:LANES] = strip[0]
        pad[1 + p, 0, :, 0:LANES] = strip[1]
        pad[side + 1, 1 + p, :, 0:LANES] = strip[2]
        pad[1 + p, side + 1, :, 0:LANES] = strip[3]
    sends_h = [
        to_sibling(rows, cols, h_send.at[n], h_recv.at[n])
        for n, (rows, cols) in enumerate(
            (
                (pl.ds(0, 1), inside),
                (inside, pl.ds(0, 1)),
                (pl.ds(side + 1, 1), inside),
                (inside, pl.ds(side + 1, 1)),
            )
        )
    ]
    for copy in sends_h:
        copy.start()
    for copy in sends_c + sends_h:
        copy.wait()

    def row(i, carry):
        a = flat(activ[i])
        total = None
        for q, (di, dj) in enumerate(((0, 0), (-1, 0), (0, -1), (1, 0), (0, 1))):
            view = flat(pad[i + 1 - di, 1 - dj : 1 - dj + side])
            term = lax.dot_general(
                view, wfull[q], (((1,), (1,)), ((), ())), preferred_element_type=F32
            )
            total = term if total is None else total + term
            acc[q] += lax.dot_general(
                a, view, (((0,), (0,)), ((), ())), preferred_element_type=F32
            )
        grad_ref[i] = (deriv[i] * total.reshape(side, tiles, ch)).astype(BF16)
        return carry

    lax.fori_loop(0, side, row, 0)

    depth = wg_ref.shape[1]
    for j in range(half_tiles):
        for k in range(2):
            part = acc[:, j * depth : (j + 1) * depth, k * LANES : (k + 1) * LANES]
            wsend[j, k] = part.astype(wsend.dtype)
    owner = chan * half_tiles
    for j in range(half_tiles):
        for k in range(2):
            there = (ens, owner + j, sec, chan if k == 0 else other)
            copy = remote(wsend.at[j, k], wrecv.at[me], g_send.at[j, k], g_recv.at[me], there)
            if k == 0:

                @pl.when(owner + j != me)
                def _():
                    copy.start()

                @pl.when(owner + j == me)
                def _():
                    wrecv[me] = wsend[j, 0]
            else:
                copy.start()
    from_chan = me // half_tiles
    for z in range(n_tile):

        @pl.when((me != z) | (from_chan != chan))
        def _():
            remote(wsend.at[0, 0], wrecv.at[z], g_send.at[0, 0], g_recv.at[z], sibling).wait_recv()

    total = wrecv[0].astype(F32)
    for z in range(1, n_tile):
        total = total + wrecv[z].astype(F32)
    wg_ref[...] = total[:, :, 0:ch] * normalizer
    for j in range(half_tiles):
        for k in range(2):
            copy = remote(wsend.at[j, k], wrecv.at[me], g_send.at[j, k], g_recv.at[me], sibling)
            if k == 0:

                @pl.when(owner + j != me)
                def _():
                    copy.wait_send()
            else:
                copy.wait_send()


def body(n_tile, n_section, activation, boundary, conv_weight, neighbours, rotations):
    _, tiles, side, _, ch = activation.shape
    taps, c_all = conv_weight.shape[1:3]
    depth = c_all // n_tile
    n_all = n_tile * tiles
    act = jnp.transpose(activation[0], (1, 2, 0, 3))
    bnd = jnp.transpose(boundary[0], (1, 2, 0, 3))
    start = lax.axis_index("tile") * tiles
    near = lax.dynamic_slice_in_dim(neighbours.T, start, tiles, 1)
    turns = lax.dynamic_slice_in_dim(rotations.T, start, tiles, 1)
    src = (jnp.arange(4, dtype=jnp.int32)[:, None] + 2 - turns) % 4
    flipped = (turns == 2) | ((turns == 1) & (src % 2 == 0)) | ((turns == 3) & (src % 2 == 1))
    idx = (src * n_all + near + jnp.where(flipped, 4 * n_all, 0)).reshape(4 * tiles, 1)
    full = side - 1
    chunks = (side - 2) // 4
    vm = pl.BlockSpec(memory_space=pltpu.VMEM)
    normalizer = float(n_all * side * side) ** -0.5
    dma = pltpu.SemaphoreType.DMA
    grad, wg = pl.pallas_call(
        functools.partial(kernel, n_tile, n_section, normalizer),
        out_shape=(
            jax.ShapeDtypeStruct((side, side, tiles, ch), BF16),
            jax.ShapeDtypeStruct((taps, depth, ch), F32),
        ),
        in_specs=[vm] * 4,
        out_specs=(vm, vm),
        scratch_shapes=[
            pltpu.VMEM((3, full, tiles, LANES), BF16),
            pltpu.VMEM((chunks, 3, side - 2, tiles, LANES), BF16),
            pltpu.VMEM((n_tile, 3, full, tiles, LANES), BF16),
            pltpu.VMEM((chunks, 3, side - 2, tiles, LANES), BF16),
            pltpu.VMEM((n_tile, full, tiles, LANES), BF16),
            pltpu.VMEM((side + 2, side + 2, tiles, 2 * LANES), BF16),
            pltpu.VMEM((taps, ch, ch), BF16),
            pltpu.VMEM((taps, ch, 2 * LANES), BF16),
            pltpu.VMEM((side, side, tiles, ch), BF16),
            pltpu.VMEM((side, side, tiles, ch), F32),
            pltpu.VMEM((taps, ch, 2 * LANES), F32),
            pltpu.VMEM((n_tile // 2, 2, taps, depth, LANES), F32),
            pltpu.VMEM((n_tile, taps, depth, LANES), F32),
            dma((1 + chunks,)),
            dma((1 + chunks,)),
            dma((n_tile - 1,)),
            dma((n_tile - 1,)),
            dma((2,)),
            dma((chunks + 2,)),
            dma((chunks + 2,)),
            dma((4,)),
            dma((4,)),
            dma((n_tile // 2, 2)),
            dma((n_tile,)),
        ],
        compiler_params=pltpu.CompilerParams(
            collective_id=0, has_side_effects=True, vmem_limit_bytes=48 * 1024 * 1024
        ),
        cost_estimate=pl.CostEstimate(
            flops=4 * taps * side * side * tiles * ch * 2 * ch,
            bytes_accessed=3 * side * side * tiles * LANES * 2,
            transcendentals=side * side * tiles * ch,
        ),
    )(act, bnd, conv_weight[0], idx)
    return jnp.transpose(grad, (2, 0, 1, 3))[None], wg[None]


def solution(mesh):
    spec = P("section", ("ens", "tile"), None, None, "chan")
    return jax.shard_map(
        functools.partial(body, mesh.shape["tile"], mesh.shape["section"]),
        mesh=mesh,
        in_specs=(spec, spec, P("section", None, None, "chan"), P(), P()),
        out_specs=(spec, P("section", "ens", "tile", "chan")),
        check_vma=False,
    )
```

time: 173 us -> 60.7 us (0.35)
  local copies, waits for them, and re-layouts: 79.2 us -> 5.26 us
  Pallas kernels: 0 us -> 52.9 us
  blocking collectives: 39.6 us -> 0 us
  matrix products: 21.3 us -> 0 us
  between operations: 14.3 us -> 0.67 us
  starting transfers between devices: 7.08 us -> 0 us
  waiting for transfers between devices: 6.71 us -> 0 us
  other arithmetic: 4.15 us -> 0.8 us
    pallas_call x0 -> x1, Pallas kernels: none -> 52.9 us  [body(): pl.pallas_call(functools.partial(kernel, n_tile, n_section, normalizer),...]
    unnamed x26 -> x8, local copies, waits for them, and re-layouts: 41.3 us -> 5.17 us
    all_gather x2 -> x0, blocking collectives: 27 us -> none  [the longest x1 24.4 us: body(): lax.all_gather(tile_edges(upstream), 'tile', axis=0, tiled=True)]
    dot_general x10 -> x0, matrix products: 21.3 us -> none  [the longest x5 15 us: body(): jnp.einsum('tijo,co->tijc', half_views[tap_index], weight_full[tap_index]...]
    convert_element_type x3 -> x0, local copies, waits for them, and re-layouts: 14.2 us -> none  [the longest x1 7.71 us: body(): half_grad = (derivative * act_grad).astype(jnp.bfloat16)]
    all_to_all x2 -> x0, blocking collectives: 12.7 us -> none  [the longest x1 8.13 us: body(): lax.all_to_all(grad_pad, 'chan', split_axis=0, concat_axis=3, tiled=True)]
    all_to_all x3 -> x0, local copies, waits for them, and re-layouts: 12.4 us -> none  [the longest x1 9.79 us: body(): lax.all_to_all(half_grad, 'chan', split_axis=3, concat_axis=0, tiled=True)]
    ppermute x1 -> x0, waiting for transfers between devices: 4.98 us -> none  [from_behind(): lax.ppermute(value, axis, [(i, (i + by) % size) for i in range(size)])]
  transfers between devices with their start and end apart: 4 -> 0, of which waited for: 2 -> 0; matrix products, arithmetic and copies ran while one was open for 45% -> 0% of each run, Pallas kernels for 0% -> 0%
where the time goes in v1:
time: 60.7 us; the launch traced here: 59.7 us
  Pallas kernels  52.9 us (87%)
  local copies, waits for them, and re-layouts  5.26 us (9%)
  other arithmetic  0.8 us (1%)
  between operations  0.67 us (1%)
    pallas_call x1, Pallas kernels, body(): pl.pallas_call(functools.partial(kernel, n_tile, n_section, normalizer),...  52.9 us
    unnamed x8, local copies, waits for them, and re-layouts  5.17 us

profile of v1, /device:TPU:1, one launch (start us, length us, event | category | flops | bytes accessed | tf_op | source)
XLA Modules:
  0.0 59.7 jit_solution(1319646901725990168)
XLA Ops:
  0.6 0.8 %fusion.2 = s32[4,24]{1,0:T(4,128)S(1)} fusion(s32[96,4]{0,1:T(4,128)} %param.8, s32[]{:T(128)S(6)} %select_n.21, s32[96,4]{0,1:T(4,128)} %param.9, s32[4]{0:T(128)S(1)} %iota_add_fusion), kind=kLoop, calls=%fused_computation.9 | loop fusion | flops 3456 | bytes 1172 | tf_op jit(solution)/shard_map/add | solution.py:290
  1.4 0.1 reshape.13.idx_ref
  1.5 0.0 copy-start
  1.6 1.3 %copy-done = bf16[1,24,14,14,96]{4,1,3,2,0:T(8,128)(2,1)S(1)} copy-done((bf16[1,24,14,14,96]{4,1,3,2,0:T(8,128)(2,1)S(1)}, bf16[1,24,14,14,96]{4,1,3,2,0:T(8,128)(2,1)}, u32[]{:S(2)}) %copy-start) | copy-done | bytes 903192
  2.8 0.0 copy-start.1
  2.8 1.3 %copy-done.1 = bf16[1,24,14,14,96]{4,1,3,2,0:T(8,128)(2,1)S(1)} copy-done((bf16[1,24,14,14,96]{4,1,3,2,0:T(8,128)(2,1)S(1)}, bf16[1,24,14,14,96]{4,1,3,2,0:T(8,128)(2,1)}, u32[]{:S(2)}) %copy-start.1) | copy-done | bytes 903192
  4.1 0.0 copy-start.2
  4.1 0.9 %copy-done.2 = bf16[1,5,192,96]{3,2,1,0:T(8,128)(2,1)S(1)} copy-done((bf16[1,5,192,96]{3,2,1,0:T(8,128)(2,1)S(1)}, bf16[1,5,192,96]{3,2,1,0:T(8,128)(2,1)}, u32[]{:S(2)}) %copy-start.2) | copy-done | bytes 184344
  5.0 52.9 %shard_map.68 = (bf16[14,14,24,96]{3,2,1,0:T(8,128)(2,1)S(1)}, f32[5,48,96]{2,1,0:T(8,128)S(1)}) custom-call(bf16[14,14,24,96]{3,2,1,0:T(8,128)(2,1)S(1)} %bitcast.35, bf16[14,14,24,96]{3,2,1,0:T(8,128)(2,1)S(1)} %bitcast.36, bf16[5,192,96]{2,1,0:T(8,128)(2,1)S(1)} %bitcast.37, s32[96,1]{1,0:T(8,128)S(1)} %reshape.13.idx_ref), custom_call_target="tpu_custom_call" | custom-call | flops 1734082560 | bytes 3612672 | tf_op jit(solution)/shard_map/pallas_call | solution.py:296
  58.0 1.0 %copy.10 = bf16[1,24,14,14,96]{4,1,3,2,0:T(8,128)(2,1)} copy(bf16[1,24,14,14,96]{4,1,3,2,0:T(8,128)(2,1)S(1)} %bitcast.33) | data formatting | bytes 1806336
  59.0 0.6 %copy.11 = f32[1,5,48,96]{3,2,1,0:T(8,128)} copy(f32[1,5,48,96]{3,2,1,0:T(8,128)S(1)} %bitcast.34) | data formatting | bytes 184320
  (1 shorter events, 0.0 us)
Async XLA Ops:
  1.5 1.3 %copy-start = (bf16[1,24,14,14,96]{4,1,3,2,0:T(8,128)(2,1)S(1)}, bf16[1,24,14,14,96]{4,1,3,2,0:T(8,128)(2,1)}, u32[]{:S(2)}) copy-start(bf16[1,24,14,14,96]{4,1,3,2,0:T(8,128)(2,1)} %param.5) | copy-start | bytes 2709508
  2.8 1.3 %copy-start.1 = (bf16[1,24,14,14,96]{4,1,3,2,0:T(8,128)(2,1)S(1)}, bf16[1,24,14,14,96]{4,1,3,2,0:T(8,128)(2,1)}, u32[]{:S(2)}) copy-start(bf16[1,24,14,14,96]{4,1,3,2,0:T(8,128)(2,1)} %param.6) | copy-start | bytes 2709508
  4.1 0.9 %copy-start.2 = (bf16[1,5,192,96]{3,2,1,0:T(8,128)(2,1)S(1)}, bf16[1,5,192,96]{3,2,1,0:T(8,128)(2,1)}, u32[]{:S(2)}) copy-start(bf16[1,5,192,96]{3,2,1,0:T(8,128)(2,1)} %param.7) | copy-start | bytes 552964

commit v2 on v1

v2 whole, which is shorter than its diff:
```python
import functools

import jax
import jax.numpy as jnp
from jax import lax
from jax.experimental import pallas as pl
from jax.experimental.pallas import tpu as pltpu
from jax.sharding import PartitionSpec as P

MESH = pl.DeviceIdType.MESH
LANES = 128
F32 = jnp.float32
BF16 = jnp.bfloat16
WIRE = jnp.float32


def flat(x):
    return x.reshape(-1, x.shape[-1])


def kernel(
    n_tile, n_section, normalizer,
    act_hbm, bnd_hbm, w_hbm, idx_ref,
    grad_ref, wg_ref,
    act_ref, bnd_ref, w_ref,
    peri_src, inner_src, ring, inner, third, pad, strips, wother, wfull, activ, deriv, totals, acc, wsend, wrecv,
    l_sem, x_send, x_recv, z_send, z_recv, w_sems, c_send, c_recv, h_send, h_recv, g_send, g_recv,
):
    ens, me, sec, chan = (lax.axis_index(a) for a in ("ens", "tile", "section", "chan"))
    side, _, tiles, ch = act_ref.shape
    full = side - 1
    half_tiles = n_tile // 2
    other = 1 - chan
    sibling = (ens, me, sec, other)
    target = (ens, me, lax.rem(sec + n_section - 1, n_section), chan)
    source = (ens, me, lax.rem(sec + 1, n_section), chan)
    lead = ch // 3
    n_chunk = inner.shape[0]

    def remote(src, dst, ss, rs, dev):
        return pltpu.make_async_remote_copy(
            src_ref=src, dst_ref=dst, send_sem=ss, recv_sem=rs, device_id=dev, device_id_type=MESH
        )

    loads = [
        pltpu.make_async_copy(src, dst, l_sem.at[n])
        for n, (src, dst) in enumerate(((bnd_hbm, bnd_ref), (w_hbm, w_ref), (act_hbm, act_ref)))
    ]
    for copy in loads:
        copy.start()
    barrier = pltpu.get_barrier_semaphore()
    for dev in (sibling, target, source):
        pl.semaphore_signal(barrier, inc=1, device_id=dev, device_id_type=MESH)
    for step in range(1, n_tile):
        for k in range(2):
            dev = (ens, lax.rem(me + step, n_tile), sec, k)
            pl.semaphore_signal(barrier, inc=1, device_id=dev, device_id_type=MESH)

    rows_i = lax.broadcasted_iota(jnp.int32, (ch, LANES), 0)
    cols_i = lax.broadcasted_iota(jnp.int32, (ch, LANES), 1)
    eye = (rows_i == cols_i).astype(BF16)
    picks = [
        ((cols_i >= ch) & (rows_i - b * lead == cols_i - ch)).astype(BF16) for b in range(3)
    ]
    wide_i = lax.broadcasted_iota(jnp.int32, (LANES, LANES), 0)
    wide_j = lax.broadcasted_iota(jnp.int32, (LANES, LANES), 1)
    moves = [
        ((wide_i >= ch) & (wide_j == wide_i - ch + b * lead)).astype(BF16) for b in range(3)
    ]

    def packed(groups, b):
        out = jnp.dot(groups[b], eye, preferred_element_type=F32) + jnp.dot(
            groups[3], picks[b], preferred_element_type=F32
        )
        return out.astype(BF16).reshape(-1, tiles, LANES)

    def untail(blocks):
        total = jnp.dot(blocks[0], moves[0], preferred_element_type=F32)
        for b in range(1, 3):
            total = total + jnp.dot(blocks[b], moves[b], preferred_element_type=F32)
        return total.astype(BF16).reshape(-1, tiles, LANES)

    def keep(x):
        lane = lax.broadcasted_iota(jnp.int32, x.shape, x.ndim - 1)
        return jnp.where(lane < ch, x.astype(F32), 0.0).astype(BF16)

    loads[0].wait()
    groups = [
        flat(bnd_ref[0, 0:full]),
        flat(bnd_ref[0:full, full]),
        flat(bnd_ref[full, 1 : full + 1]),
        flat(bnd_ref[1 : full + 1, 0]),
    ]
    sends_peri = []
    for b in range(3):
        peri_src[b] = packed(groups, b)
        if b == 0:
            pl.semaphore_wait(barrier, 3 + 2 * (n_tile - 1))
        copy = remote(peri_src.at[b], ring.at[me, b], x_send.at[b], x_recv.at[b], target)
        copy.start()
        sends_peri.append(copy)
    loads[1].wait()
    mine_c = pl.multiple_of(chan * ch, 16)
    other_c = pl.multiple_of(other * ch, 16)
    send_w = remote(w_ref.at[:, pl.ds(other_c, ch), :], wother, w_sems.at[0], w_sems.at[1], sibling)
    send_w.start()
    sends_inner = []
    for m in range(n_chunk):
        first = 1 + 4 * m
        groups = [flat(bnd_ref[first + g, 1:full]) for g in range(4)]
        for b in range(3):
            inner_src[m, b] = packed(groups, b)
        sends_inner.append(
            remote(inner_src.at[m], inner.at[m], x_send.at[3 + m], x_recv.at[3 + m], target)
        )
    sends_z = []
    for b in range(3):
        sends_peri[b].wait()
        if b == 0:
            sends_inner[0].start()
        for step in range(1, n_tile):
            dev = (ens, lax.rem(me + step, n_tile), sec, chan)
            copy = remote(
                ring.at[me, b], ring.at[me, b], z_send.at[step - 1, b], z_recv.at[step - 1, b], dev
            )
            copy.start()
            sends_z.append(copy)
    sends_inner[1].start()

    blocks = [ring[me, b] for b in range(3)]
    pad[1, 1 : full + 1, :, 0:LANES] = keep(blocks[0])
    pad[1 : full + 1, full + 1, :, 0:LANES] = keep(blocks[1])
    pad[full + 1, 2 : full + 2, :, 0:LANES] = keep(blocks[2])
    pad[2 : full + 2, 1, :, 0:LANES] = untail([flat(x) for x in blocks])

    def to_sibling(rows, cols, ss, rs):
        return remote(
            pad.at[rows, cols, :, 0:LANES], pad.at[rows, cols, :, LANES : 2 * LANES], ss, rs, sibling
        )

    inside = pl.ds(1, side)
    sends_c = [
        to_sibling(pl.ds(first, 1), inside, c_send.at[n_chunk + n], c_recv.at[n_chunk + n])
        for n, first in enumerate((1, side))
    ]
    for copy in sends_c:
        copy.start()

    none = jnp.zeros((side, tiles, 2 * LANES), BF16)
    pad[0, 1 : side + 1] = none
    pad[side + 1, 1 : side + 1] = none
    pad[1 : side + 1, 0] = none
    pad[1 : side + 1, side + 1] = none
    acc[...] = jnp.zeros_like(acc)
    wfull[...] = jnp.zeros_like(wfull)
    wfull[:, :, 0:ch] = w_ref[:, pl.ds(mine_c, ch), :]
    send_w.wait()
    wfull[:, :, LANES : LANES + ch] = wother[...]

    loads[2].wait()

    def silu_row(i, carry):
        v = act_ref[i].astype(F32)
        logistic = 1.0 / (1.0 + jnp.exp(-v))
        activ[i] = (v * logistic).astype(BF16)
        deriv[i] = logistic * (1.0 + v * (1.0 - logistic))
        return carry

    lax.fori_loop(0, side, silu_row, 0)

    def times(view, q):
        return lax.dot_general(
            view, wfull[q], (((1,), (1,)), ((), ())), preferred_element_type=F32
        )

    def against(a, view):
        return lax.dot_general(a, view, (((0,), (0,)), ((), ())), preferred_element_type=F32)

    def row(i, carry):
        a = flat(activ[i])
        total = None
        for q, (di, dj) in enumerate(((0, 0), (-1, 0), (0, -1), (1, 0), (0, 1))):
            view = flat(pad[i + 1 - di, 1 - dj : 1 - dj + side])
            term = times(view, q)
            total = term if total is None else total + term
            acc[q] += against(a, view)
        total = total.reshape(side, tiles, ch)
        totals[i] = total
        grad_ref[i] = (deriv[i] * total).astype(BF16)
        return carry

    for m in range(n_chunk):
        sends_inner[m].wait()
        if m + 2 < n_chunk:
            sends_inner[m + 2].start()
        first = 2 + 4 * m
        blocks = [inner[m, b] for b in range(3)]
        for b in range(3):
            pad[first + b, 2 : full + 1, :, 0:LANES] = keep(blocks[b])
        pad[first + 3, 2 : full + 1, :, 0:LANES] = untail([flat(x) for x in blocks])
        copy = to_sibling(pl.ds(first, 4), inside, c_send.at[m], c_recv.at[m])
        copy.start()
        if m == 0:
            for early in sends_c:
                early.wait()
        copy.wait()
        lax.fori_loop(4 * m, 4 * m + 4 if m + 1 < n_chunk else side, row, 0)

    depth = wg_ref.shape[1]
    owner = chan * half_tiles

    def share(part, q0, q1):
        for j in range(half_tiles):
            for k in range(2):
                wsend[j, k, q0:q1] = acc[
                    q0:q1, j * depth : (j + 1) * depth, k * LANES : (k + 1) * LANES
                ].astype(wsend.dtype)
                copy = outgoing(part, q0, q1, j, k)
                if k == 0:

                    @pl.when(owner + j != me)
                    def _():
                        copy.start()

                    @pl.when(owner + j == me)
                    def _():
                        wrecv[me, q0:q1] = wsend[j, 0, q0:q1]
                else:
                    copy.start()

    def outgoing(part, q0, q1, j, k):
        there = (ens, owner + j, sec, chan if k == 0 else other)
        return remote(
            wsend.at[j, k, q0:q1], wrecv.at[me, q0:q1], g_send.at[part, j, k], g_recv.at[part, me], there
        )

    n_tap = acc.shape[0]
    parts = ((0, 1), (1, n_tap))
    share(0, *parts[0])

    for copy in sends_z:
        copy.wait()
    for z in range(n_tile):
        third[z] = untail([flat(ring[z, b]) for b in range(3)])

    def edge(s, p):
        if s == 0:
            part = ring[:, 0, p] if p < full else ring[:, 1, 0]
        elif s == 3:
            part = ring[:, 1, p] if p < full else ring[:, 2, full - 1]
        elif s == 2:
            part = third[:, full - 1] if p == 0 else ring[:, 2, p - 1]
        else:
            part = ring[:, 0, 0] if p == 0 else third[:, p - 1]
        return flat(part)

    n_all = n_tile * tiles
    which = idx_ref[...]
    spots = lax.broadcasted_iota(jnp.int32, (4 * tiles, 4 * n_all), 1)
    plain = (which == spots).astype(F32).astype(BF16)
    turned = (which == spots + 4 * n_all).astype(F32).astype(BF16)
    for p in range(side):
        ahead = jnp.concatenate([edge(s, p) for s in range(4)], axis=0)
        behind = jnp.concatenate([edge(s, full - p) for s in range(4)], axis=0)
        strip = jnp.dot(plain, ahead, preferred_element_type=F32) + jnp.dot(
            turned, behind, preferred_element_type=F32
        )
        strips[:, p, :, 0:LANES] = keep(strip).reshape(4, tiles, LANES)
    send_h = remote(
        strips.at[:, :, :, 0:LANES], strips.at[:, :, :, LANES : 2 * LANES], h_send.at[0], h_recv.at[0], sibling
    )
    send_h.start()
    send_h.wait()
    taps_of = (3, 4, 1, 2)
    for k, q in enumerate(taps_of):
        a = (activ[0], activ[:, 0], activ[full], activ[:, full])[k]
        acc[q] += against(flat(a), flat(strips[k]))
    share(1, *parts[1])
    for k, q in enumerate(taps_of):
        term = times(flat(strips[k]), q).reshape(side, tiles, ch)
        if k == 0:
            totals[0] += term
        elif k == 1:
            totals[:, 0] += term
        elif k == 2:
            totals[full] += term
        else:
            totals[:, full] += term
    grad_ref[0] = (deriv[0] * totals[0]).astype(BF16)
    grad_ref[full] = (deriv[full] * totals[full]).astype(BF16)
    grad_ref[1:full, 0] = (deriv[1:full, 0] * totals[1:full, 0]).astype(BF16)
    grad_ref[1:full, full] = (deriv[1:full, full] * totals[1:full, full]).astype(BF16)

    from_chan = me // half_tiles
    for part, (q0, q1) in enumerate(parts):
        for z in range(n_tile):

            @pl.when((me != z) | (from_chan != chan))
            def _():
                remote(
                    wsend.at[0, 0, q0:q1], wrecv.at[z, q0:q1], g_send.at[part, 0, 0], g_recv.at[part, z], sibling
                ).wait_recv()

    total = wrecv[0].astype(F32)
    for z in range(1, n_tile):
        total = total + wrecv[z].astype(F32)
    wg_ref[...] = total[:, :, 0:ch] * normalizer
    for part, (q0, q1) in enumerate(parts):
        for j in range(half_tiles):
            for k in range(2):
                copy = outgoing(part, q0, q1, j, k)
                if k == 0:

                    @pl.when(owner + j != me)
                    def _():
                        copy.wait_send()
                else:
                    copy.wait_send()


def body(n_tile, n_section, activation, boundary, conv_weight, neighbours, rotations):
    _, tiles, side, _, ch = activation.shape
    taps, c_all = conv_weight.shape[1:3]
    depth = c_all // n_tile
    n_all = n_tile * tiles
    act = jnp.transpose(activation[0], (1, 2, 0, 3))
    bnd = jnp.transpose(boundary[0], (1, 2, 0, 3))
    start = lax.axis_index("tile") * tiles
    near = lax.dynamic_slice_in_dim(neighbours.T, start, tiles, 1)
    turns = lax.dynamic_slice_in_dim(rotations.T, start, tiles, 1)
    src = (jnp.arange(4, dtype=jnp.int32)[:, None] + 2 - turns) % 4
    flipped = (turns == 2) | ((turns == 1) & (src % 2 == 0)) | ((turns == 3) & (src % 2 == 1))
    idx = (src * n_all + near + jnp.where(flipped, 4 * n_all, 0)).reshape(4 * tiles, 1)
    full = side - 1
    chunks = (side - 2) // 4
    vm = pl.BlockSpec(memory_space=pltpu.VMEM)
    normalizer = float(n_all * side * side) ** -0.5
    dma = pltpu.SemaphoreType.DMA
    grad, wg = pl.pallas_call(
        functools.partial(kernel, n_tile, n_section, normalizer),
        out_shape=(
            jax.ShapeDtypeStruct((side, side, tiles, ch), BF16),
            jax.ShapeDtypeStruct((taps, depth, ch), F32),
        ),
        in_specs=[pl.BlockSpec(memory_space=pl.ANY)] * 3 + [vm],
        out_specs=(vm, vm),
        scratch_shapes=[
            pltpu.VMEM((side, side, tiles, ch), BF16),
            pltpu.VMEM((side, side, tiles, ch), BF16),
            pltpu.VMEM((taps, c_all, ch), BF16),
            pltpu.VMEM((3, full, tiles, LANES), BF16),
            pltpu.VMEM((chunks, 3, side - 2, tiles, LANES), BF16),
            pltpu.VMEM((n_tile, 3, full, tiles, LANES), BF16),
            pltpu.VMEM((chunks, 3, side - 2, tiles, LANES), BF16),
            pltpu.VMEM((n_tile, full, tiles, LANES), BF16),
            pltpu.VMEM((side + 2, side + 2, tiles, 2 * LANES), BF16),
            pltpu.VMEM((4, side, tiles, 2 * LANES), BF16),
            pltpu.VMEM((taps, ch, ch), BF16),
            pltpu.VMEM((taps, ch, 2 * LANES), BF16),
            pltpu.VMEM((side, side, tiles, ch), BF16),
            pltpu.VMEM((side, side, tiles, ch), F32),
            pltpu.VMEM((side, side, tiles, ch), F32),
            pltpu.VMEM((taps, ch, 2 * LANES), F32),
            pltpu.VMEM((n_tile // 2, 2, taps, depth, LANES), WIRE),
            pltpu.VMEM((n_tile, taps, depth, LANES), WIRE),
            dma((3,)),
            dma((3 + chunks,)),
            dma((3 + chunks,)),
            dma((n_tile - 1, 3)),
            dma((n_tile - 1, 3)),
            dma((2,)),
            dma((chunks + 2,)),
            dma((chunks + 2,)),
            dma((1,)),
            dma((1,)),
            dma((2, n_tile // 2, 2)),
            dma((2, n_tile)),
        ],
        compiler_params=pltpu.CompilerParams(
            collective_id=0, has_side_effects=True, vmem_limit_bytes=48 * 1024 * 1024
        ),
        cost_estimate=pl.CostEstimate(
            flops=4 * taps * side * side * tiles * ch * 2 * ch,
            bytes_accessed=3 * side * side * tiles * LANES * 2,
            transcendentals=side * side * tiles * ch,
        ),
    )(act, bnd, conv_weight[0], idx)
    return jnp.transpose(grad, (2, 0, 1, 3))[None], wg[None]


def solution(mesh):
    spec = P("section", ("ens", "tile"), None, None, "chan")
    return jax.shard_map(
        functools.partial(body, mesh.shape["tile"], mesh.shape["section"]),
        mesh=mesh,
        in_specs=(spec, spec, P("section", None, None, "chan"), P(), P()),
        out_specs=(spec, P("section", "ens", "tile", "chan")),
        check_vma=False,
    )
```

time: 60.7 us -> 51.3 us (0.85)
  Pallas kernels: 52.9 us -> 44 us
    pallas_call x1, Pallas kernels: 52.9 us -> 44 us  [body(): pl.pallas_call(functools.partial(kernel, n_tile, n_section, normalizer),...]
where the time goes in v2:
time: 51.3 us; the launch traced here: 50.8 us
  Pallas kernels  44 us (86%)
  local copies, waits for them, and re-layouts  5.26 us (10%)
  other arithmetic  0.8 us (2%)
  between operations  0.67 us (1%)
    pallas_call x1, Pallas kernels, body(): pl.pallas_call(functools.partial(kernel, n_tile, n_section, normalizer),...  44 us
    unnamed x8, local copies, waits for them, and re-layouts  5.17 us

profile of v2, /device:TPU:1, one launch (start us, length us, event | category | flops | bytes accessed | tf_op | source)
XLA Modules:
  0.0 50.8 jit_solution(392488630836757658)
XLA Ops:
  0.6 0.8 %fusion.2 = s32[4,24]{1,0:T(4,128)S(1)} fusion(s32[96,4]{0,1:T(4,128)} %param.8, s32[]{:T(128)S(6)} %select_n.21, s32[96,4]{0,1:T(4,128)} %param.9, s32[4]{0:T(128)S(1)} %iota_add_fusion), kind=kLoop, calls=%fused_computation.9 | loop fusion | flops 3456 | bytes 1172 | tf_op jit(solution)/shard_map/add | solution.py:333
  1.4 0.1 reshape.13.idx_ref
  1.5 0.0 copy-start
  1.6 1.3 %copy-done = bf16[1,24,14,14,96]{4,1,3,2,0:T(8,128)(2,1)S(1)} copy-done((bf16[1,24,14,14,96]{4,1,3,2,0:T(8,128)(2,1)S(1)}, bf16[1,24,14,14,96]{4,1,3,2,0:T(8,128)(2,1)}, u32[]{:S(2)}) %copy-start) | copy-done | bytes 903192
  2.8 0.0 copy-start.1
  2.8 1.3 %copy-done.1 = bf16[1,24,14,14,96]{4,1,3,2,0:T(8,128)(2,1)S(1)} copy-done((bf16[1,24,14,14,96]{4,1,3,2,0:T(8,128)(2,1)S(1)}, bf16[1,24,14,14,96]{4,1,3,2,0:T(8,128)(2,1)}, u32[]{:S(2)}) %copy-start.1) | copy-done | bytes 903192
  4.1 0.0 copy-start.2
  4.1 0.9 %copy-done.2 = bf16[1,5,192,96]{3,2,1,0:T(8,128)(2,1)S(1)} copy-done((bf16[1,5,192,96]{3,2,1,0:T(8,128)(2,1)S(1)}, bf16[1,5,192,96]{3,2,1,0:T(8,128)(2,1)}, u32[]{:S(2)}) %copy-start.2) | copy-done | bytes 184344
  5.0 44.0 %shard_map.68 = (bf16[14,14,24,96]{3,2,1,0:T(8,128)(2,1)S(1)}, f32[5,48,96]{2,1,0:T(8,128)S(1)}) custom-call(bf16[14,14,24,96]{3,2,1,0:T(8,128)(2,1)S(1)} %bitcast.35, bf16[14,14,24,96]{3,2,1,0:T(8,128)(2,1)S(1)} %bitcast.36, bf16[5,192,96]{2,1,0:T(8,128)(2,1)S(1)} %bitcast.37, s32[96,1]{1,0:T(8,128)S(1)} %reshape.13.idx_ref), custom_call_target="tpu_custom_call" | custom-call | flops 1734082560 | bytes 3612672 | tf_op jit(solution)/shard_map/pallas_call | solution.py:339
  49.1 1.0 %copy.10 = bf16[1,24,14,14,96]{4,1,3,2,0:T(8,128)(2,1)} copy(bf16[1,24,14,14,96]{4,1,3,2,0:T(8,128)(2,1)S(1)} %bitcast.33) | data formatting | bytes 1806336
  50.1 0.6 %copy.11 = f32[1,5,48,96]{3,2,1,0:T(8,128)} copy(f32[1,5,48,96]{3,2,1,0:T(8,128)S(1)} %bitcast.34) | data formatting | bytes 184320
  (1 shorter events, 0.0 us)
Async XLA Ops:
  1.5 1.3 %copy-start = (bf16[1,24,14,14,96]{4,1,3,2,0:T(8,128)(2,1)S(1)}, bf16[1,24,14,14,96]{4,1,3,2,0:T(8,128)(2,1)}, u32[]{:S(2)}) copy-start(bf16[1,24,14,14,96]{4,1,3,2,0:T(8,128)(2,1)} %param.5) | copy-start | bytes 2709508
  2.8 1.3 %copy-start.1 = (bf16[1,24,14,14,96]{4,1,3,2,0:T(8,128)(2,1)S(1)}, bf16[1,24,14,14,96]{4,1,3,2,0:T(8,128)(2,1)}, u32[]{:S(2)}) copy-start(bf16[1,24,14,14,96]{4,1,3,2,0:T(8,128)(2,1)} %param.6) | copy-start | bytes 2709508
  4.1 0.9 %copy-start.2 = (bf16[1,5,192,96]{3,2,1,0:T(8,128)(2,1)S(1)}, bf16[1,5,192,96]{3,2,1,0:T(8,128)(2,1)}, u32[]{:S(2)}) copy-start(bf16[1,5,192,96]{3,2,1,0:T(8,128)(2,1)} %param.7) | copy-start | bytes 552964

commit v3 on v2

--- a/solution.py
+++ b/solution.py
@@ -11,7 +11,7 @@
 LANES = 128
 F32 = jnp.float32
 BF16 = jnp.bfloat16
-WIRE = jnp.float32
+WIRE = jnp.bfloat16
 
 
 def flat(x):
@@ -99,25 +99,18 @@
         copy = remote(peri_src.at[b], ring.at[me, b], x_send.at[b], x_recv.at[b], target)
         copy.start()
         sends_peri.append(copy)
-    loads[1].wait()
-    mine_c = pl.multiple_of(chan * ch, 16)
-    other_c = pl.multiple_of(other * ch, 16)
-    send_w = remote(w_ref.at[:, pl.ds(other_c, ch), :], wother, w_sems.at[0], w_sems.at[1], sibling)
-    send_w.start()
-    sends_inner = []
-    for m in range(n_chunk):
+    def ready(m):
         first = 1 + 4 * m
         groups = [flat(bnd_ref[first + g, 1:full]) for g in range(4)]
         for b in range(3):
             inner_src[m, b] = packed(groups, b)
-        sends_inner.append(
-            remote(inner_src.at[m], inner.at[m], x_send.at[3 + m], x_recv.at[3 + m], target)
-        )
+        return remote(inner_src.at[m], inner.at[m], x_send.at[3 + m], x_recv.at[3 + m], target)
+
+    sends_inner = [ready(0)]
+    sends_inner[0].start()
     sends_z = []
     for b in range(3):
         sends_peri[b].wait()
-        if b == 0:
-            sends_inner[0].start()
         for step in range(1, n_tile):
             dev = (ens, lax.rem(me + step, n_tile), sec, chan)
             copy = remote(
@@ -125,7 +118,14 @@
             )
             copy.start()
             sends_z.append(copy)
-    sends_inner[1].start()
+    for m in range(1, n_chunk):
+        sends_inner.append(ready(m))
+        sends_inner[m].start()
+    loads[1].wait()
+    mine_c = pl.multiple_of(chan * ch, 16)
+    other_c = pl.multiple_of(other * ch, 16)
+    send_w = remote(w_ref.at[:, pl.ds(other_c, ch), :], wother, w_sems.at[0], w_sems.at[1], sibling)
+    send_w.start()
 
     blocks = [ring[me, b] for b in range(3)]
     pad[1, 1 : full + 1, :, 0:LANES] = keep(blocks[0])
@@ -191,8 +191,6 @@
 
     for m in range(n_chunk):
         sends_inner[m].wait()
-        if m + 2 < n_chunk:
-            sends_inner[m + 2].start()
         first = 2 + 4 * m
         blocks = [inner[m, b] for b in range(3)]
         for b in range(3):
@@ -342,7 +340,7 @@
             jax.ShapeDtypeStruct((side, side, tiles, ch), BF16),
             jax.ShapeDtypeStruct((taps, depth, ch), F32),
         ),
-        in_specs=[pl.BlockSpec(memory_space=pl.ANY)] * 3 + [vm],
+        in_specs=[pl.BlockSpec(memory_space=pltpu.HBM)] * 3 + [vm],
         out_specs=(vm, vm),
         scratch_shapes=[
             pltpu.VMEM((side, side, tiles, ch), BF16),
@@ -377,7 +375,7 @@
             dma((2, n_tile)),
         ],
         compiler_params=pltpu.CompilerParams(
-            collective_id=0, has_side_effects=True, vmem_limit_bytes=48 * 1024 * 1024
+            collective_id=0, has_side_effects=True, vmem_limit_bytes=60 * 1024 * 1024
         ),
         cost_estimate=pl.CostEstimate(
             flops=4 * taps * side * side * tiles * ch * 2 * ch,

time: 51.3 us -> 47.5 us (0.926)
  Pallas kernels: 44 us -> 41.8 us
  local copies, waits for them, and re-layouts: 5.26 us -> 3.91 us
    pallas_call x1, Pallas kernels: 44 us -> 41.8 us  [body(): pl.pallas_call(functools.partial(kernel, n_tile, n_section, normalizer),...]
    unnamed x8 -> x4, local copies, waits for them, and re-layouts: 5.17 us -> 3.19 us
    reshape x1, local copies, waits for them, and re-layouts: 0.09 us -> 0.72 us  [body(): (src * n_all + near + jnp.where(flipped, 4 * n_all, 0)).reshape(4 * tiles...]
where the time goes in v3:
time: 47.5 us; the launch traced here: 47.2 us
  Pallas kernels  41.8 us (88%)
  local copies, waits for them, and re-layouts  3.91 us (8%)
  other arithmetic  0.8 us (2%)
  between operations  0.66 us (1%)
    pallas_call x1, Pallas kernels, body(): pl.pallas_call(functools.partial(kernel, n_tile, n_section, normalizer),...  41.8 us
    unnamed x4, local copies, waits for them, and re-layouts  3.19 us

profile of v3, /device:TPU:1, one launch (start us, length us, event | category | flops | bytes accessed | tf_op | source)
XLA Modules:
  0.0 47.2 jit_solution(849854421242211189)
XLA Ops:
  0.6 0.8 %fusion.2 = s32[4,24]{1,0:T(4,128)S(1)} fusion(s32[96,4]{0,1:T(4,128)} %param.8, s32[]{:T(128)S(6)} %select_n.21, s32[96,4]{0,1:T(4,128)} %param.9, s32[4]{0:T(128)S(1)} %iota_add_fusion), kind=kLoop, calls=%fused_computation.9 | loop fusion | flops 3456 | bytes 1172 | tf_op jit(solution)/shard_map/add | solution.py:331
  1.4 0.7 %reshape.13.idx_ref = s32[96,1]{1,0:T(8,128)} reshape(s32[4,24]{1,0:T(4,128)S(1)} %fusion.2) | data formatting | bytes 768 | tf_op jit(solution)/shard_map/reshape | solution.py:331
  2.2 41.8 %shard_map.68 = (bf16[14,14,24,96]{3,2,1,0:T(8,128)(2,1)}, f32[5,48,96]{2,1,0:T(8,128)}) custom-call(bf16[14,14,24,96]{3,2,1,0:T(8,128)(2,1)} %bitcast.35, bf16[14,14,24,96]{3,2,1,0:T(8,128)(2,1)} %bitcast.36, bf16[5,192,96]{2,1,0:T(8,128)(2,1)} %bitcast.37, s32[96,1]{1,0:T(8,128)} %reshape.13.idx_ref), custom_call_target="tpu_custom_call" | custom-call | flops 1734082560 | bytes 3612672 | tf_op jit(solution)/shard_map/pallas_call | solution.py:337
  44.0 0.0 copy-start
  44.0 2.5 %copy.10 = bf16[1,24,14,14,96]{4,1,3,2,0:T(8,128)(2,1)} copy(bf16[1,24,14,14,96]{4,1,3,2,0:T(8,128)(2,1)} %bitcast.33) | data formatting | bytes 1806336
  46.6 0.0 copy-done
  46.6 0.6 %copy.11 = f32[1,5,48,96]{3,2,1,0:T(8,128)} copy(f32[1,5,48,96]{3,2,1,0:T(8,128)S(1)} %bitcast.34) | data formatting | bytes 184320
  (1 shorter events, 0.0 us)
Async XLA Ops:
  44.0 2.6 %copy-start = (f32[5,48,96]{2,1,0:T(8,128)S(1)}, f32[5,48,96]{2,1,0:T(8,128)}, u32[]{:S(2)}) copy-start(f32[5,48,96]{2,1,0:T(8,128)} %get-tuple-element.5) | copy-start | bytes 276484
